TPU v7x, 128 devices: a whole 4x4x4 slice. The times are simulated.
128 devices in a mesh: row: 32 (over y, z, x_hi), col: 4 (over x_lo, core).
Axes of the slice: x: 4 (x_hi: 2, x_lo: 2; x = x_hi * 2 + x_lo), y: 4, z: 4, core: 2. Of those that a mesh axis runs over, the one named last changes fastest.
Arguments:
- hidden_in: bfloat16 [16384, 1024], P('row', 'col'), may hold values from -6 to 6
- segment_ids: int32 [16384], P('row'), may hold values from 0 to 3, as said below
- cotangent: bfloat16 [16384, 1024], P('row', 'col'), may hold values from -6 to 6
- w_in: bfloat16 [1, 1024, 4120], P(None, 'row', 'col'), may hold values from -0.1875 to 0.1875
- w_out: bfloat16 [1, 2048, 1024], P(None, 'col', 'row'), may hold values from -0.1875 to 0.1875
- w_gate_up: bfloat16 [1, 1024, 4096], P(None, 'row', 'col'), may hold values from -0.1875 to 0.1875
- w_down: bfloat16 [1, 2048, 1024], P(None, 'col', 'row'), may hold values from -0.125 to 0.125
- norm_gains: float32 [1, 2, 1024], P(None, None, 'col'), may hold values from 0.5 to 1.5
- ssm_gain: float32 [1, 1536], P(None, 'col'), may hold values from 0.5 to 1.5
- head_params: float32 [1, 3, 24], P(None, None, 'col'), may hold values from -7 to 3
- conv_weight: float32 [1, 4, 1792], P(None, None, 'col'), may hold values from -3 to 3
- conv_bias: float32 [1, 1792], P(None, 'col'), may hold values from -3 to 3
Outputs:
- hidden_out: bfloat16 [16384, 1024], P('row', 'col')
- grad_hidden: float32 [16384, 1024], P('row', 'col')
- grad_w_in: float32 [1, 1024, 4120], P(None, 'row', 'col')
- grad_w_out: float32 [1, 2048, 1024], P(None, 'col', 'row')
- grad_w_gate_up: float32 [1, 1024, 4096], P(None, 'row', 'col')
- grad_w_down: float32 [1, 2048, 1024], P(None, 'col', 'row')
- grad_norm_gains: float32 [1, 2, 1024], P(None, None, 'col')
- grad_ssm_gain: float32 [1, 1536], P(None, 'col')
- grad_head_params: float32 [1, 3, 24], P(None, None, 'col')
- grad_conv_weight: float32 [1, 4, 1792], P(None, None, 'col')
- grad_conv_bias: float32 [1, 1792], P(None, 'col')
Inputs may be any that keep to these rules, and one draw needn't show every extreme that they name: `segment_ids`: within each sequence of 512 tokens the ids start at 0, never fall, rise by one at each step up, and end at 3.
All inputs are finite; a program needn't handle non-finite values.
Results may differ from a plain program's by a relative error of at most 0.024.
Values may be sent and summed in bfloat16 or wider, within the bound.
No kernel may reach another device: no remote copies, remote signals or barrier semaphores. Data moves between devices by JAX's collectives and lax.ppermute only.
A program may use at most 128 MiB of HBM per device.

v0:
```python
import jax
import jax.numpy as jnp
from jax import lax
from jax.sharding import PartitionSpec as P

D = 1024
Q_HEADS = 8
KV_HEADS = 2
HEAD = 64
SSM_HEADS = 24
SSM_HEAD = 64
STATE = 128
CONV = 4
FF = 2048
LAYERS = 1


epsilon = 1e-05
rope_base = 10000.0
contract_last = (((1,), (1,)), ((), ()))
contract_first = (((0,), (0,)), ((), ()))


def lowered(value):
    rounded = lax.optimization_barrier(value.astype(jnp.bfloat16)).astype(jnp.float32)
    return value + lax.stop_gradient(rounded - value)


def sequence_masks(segments):
    length = segments.shape[0]
    index = jnp.arange(length, dtype=jnp.int32)
    previous = jnp.concatenate([segments[:1], segments[:-1]])
    starts = jnp.where(segments != previous, index, 0)
    positions = (index - lax.cummax(starts, axis=0)).astype(jnp.float32)
    allowed = (segments[:, None] == segments[None, :]) & (index[:, None] >= index[None, :])
    shifted = []
    for shift in range(CONV):
        earlier = jnp.concatenate([jnp.full((shift,), -1, jnp.int32), segments[: length - shift]])
        shifted.append((earlier == segments).astype(jnp.float32))
    return (positions, allowed, jnp.stack(shifted))


def rotate(values, positions):
    middle = values.shape[-1] // 2
    frequency = rope_base ** (-2.0 * jnp.arange(middle, dtype=jnp.float32) / values.shape[-1])
    angle = positions[:, None] * frequency[None, :]
    cosine = jnp.cos(angle)[:, None, :]
    sine = jnp.sin(angle)[:, None, :]
    first = values[..., :middle]
    second = values[..., middle:]
    return jnp.concatenate([first * cosine - second * sine, second * cosine + first * sine], -1)


def causal_conv(inner, weight, bias, valid):
    length = inner.shape[0]
    running = jnp.broadcast_to(bias[None, :], inner.shape)
    for shift in range(CONV):
        earlier = jnp.concatenate(
            [jnp.zeros((shift, inner.shape[1]), inner.dtype), inner[: length - shift]]
        )
        running = running + weight[shift][None, :] * earlier * valid[shift][:, None]
    return running


def conv_section(block, weight, bias, valid, widths):
    query_cols, ssm_cols, state_cols, head_cols = widths
    start_kv = query_cols + 2 * ssm_cols
    inner = jnp.concatenate(
        [
            block[:, query_cols + ssm_cols : start_kv],
            block[:, start_kv + HEAD : start_kv + HEAD + state_cols],
        ],
        1,
    )
    active = jax.nn.silu(causal_conv(inner, weight, bias, valid))
    sent = jnp.concatenate(
        [lowered(block[:, start_kv : start_kv + HEAD]), lowered(active[:, ssm_cols:])], 1
    )
    return (active[:, :ssm_cols], sent)


def mixer_core(block, convolved, shared, params, positions, allowed, column, widths):
    query_cols, ssm_cols, state_cols, head_cols = widths
    length = block.shape[0]
    col_count = shared.shape[1] // (HEAD + state_cols)
    pieces = shared.reshape(length, col_count, HEAD + state_cols)
    key_index = column * KV_HEADS // col_count
    keys = lax.dynamic_index_in_dim(pieces[:, :KV_HEADS, :HEAD], key_index, 1, keepdims=False)
    values = lax.dynamic_index_in_dim(pieces[:, KV_HEADS:, :HEAD], key_index, 1, keepdims=False)
    states = pieces[:, :, HEAD:].reshape(length, col_count * state_cols)
    state_b = states[:, :STATE]
    state_c = states[:, STATE:]
    query = block[:, :query_cols].reshape(length, query_cols // HEAD, HEAD)
    qrot = lowered(rotate(query, positions))
    krot = lowered(rotate(keys[:, None, :], positions))[:, 0]
    scores = jnp.einsum("shd,td->hst", qrot, krot) * HEAD ** (-0.5)
    scores = jnp.where(allowed[None], scores, -1e30)
    top = jnp.max(scores, axis=-1, keepdims=True)
    weights = jnp.exp(scores - top)
    probs = lowered(weights / jnp.sum(weights, axis=-1, keepdims=True))
    attn = lowered(jnp.einsum("hst,td->shd", probs, values)).reshape(length, query_cols)
    gate_z = block[:, query_cols : query_cols + ssm_cols]
    step_size = jax.nn.softplus(block[:, block.shape[1] - head_cols :] + params[2][None, :])
    logdecay = jnp.cumsum(step_size * (-jnp.exp(params[0]))[None, :], axis=0).T
    gram = jnp.dot(state_c, state_b.T)
    diff = logdecay[:, :, None] - logdecay[:, None, :]
    mixing = lowered(
        jnp.where(allowed[None], jnp.exp(jnp.where(allowed[None], diff, 0.0)), 0.0) * gram[None]
    )
    xin = convolved.reshape(length, head_cols, SSM_HEAD)
    inputs = lowered(step_size[:, :, None] * xin)
    ssm = jnp.einsum("hts,shp->thp", mixing, inputs) + params[1][None, :, None] * xin
    gated = ssm.reshape(length, ssm_cols) * jax.nn.silu(gate_z)
    return (attn, gated)


def per_device(
    hidden_in,
    segment_ids,
    cotangent,
    w_in,
    w_out,
    w_gate_up,
    w_down,
    norm_gains,
    ssm_gain,
    head_params,
    conv_weight,
    conv_bias,
):
    col_count = lax.axis_size("col")
    column = lax.axis_index("col")
    widths = (
        Q_HEADS * HEAD // col_count,
        SSM_HEADS * SSM_HEAD // col_count,
        2 * STATE // col_count,
        SSM_HEADS // col_count,
    )
    query_cols = widths[0]
    ffn_cols = FF // col_count
    ssm_width = SSM_HEADS * SSM_HEAD
    shard_rows = w_in.shape[1]
    positions, allowed, valid = sequence_masks(segment_ids)

    def row_total(values):
        return lax.psum(values, "col")

    def features(values):
        return lax.all_gather(values, "col", axis=1, tiled=True)

    def feature_sum(values):
        return lax.psum_scatter(values, "col", scatter_dimension=1, tiled=True)

    def weight_grad_rows(left, grad):

        def term(start, count):
            return lax.dot_general(left, grad, contract_first, preferred_element_type=jnp.float32)

        return lax.psum_scatter(
            term(jnp.int32(0), lax.axis_size("row") * shard_rows).astype(jnp.bfloat16),
            "row",
            scatter_dimension=0,
            tiled=True,
        ).astype(jnp.float32)

    def weight_grad_cols(left, grad):
        term = lax.dot_general(left, grad, contract_first, preferred_element_type=jnp.float32)
        return lax.psum_scatter(
            term.astype(jnp.bfloat16), "row", scatter_dimension=1, tiled=True
        ).astype(jnp.float32)

    def forward_in(left, second, layer_index):
        weight = (w_in, w_gate_up)[second][layer_index]
        return jnp.dot(
            left,
            lax.all_gather(weight, "row", axis=0, tiled=True),
            preferred_element_type=jnp.float32,
        )

    def forward_out(left, second, layer_index):
        weight = (w_out, w_down)[second][layer_index]
        return jnp.dot(
            left,
            lax.all_gather(weight, "row", axis=1, tiled=True),
            preferred_element_type=jnp.float32,
        )

    def back_out(grad, second, layer_index):
        weight = (w_out, w_down)[second][layer_index]
        return lax.dot_general(
            grad,
            lax.all_gather(weight, "row", axis=1, tiled=True),
            contract_last,
            preferred_element_type=jnp.float32,
        )

    def back_in(grad, second, layer_index):
        weight = (w_in, w_gate_up)[second][layer_index]
        return lax.dot_general(
            grad,
            lax.all_gather(weight, "row", axis=0, tiled=True),
            contract_last,
            preferred_element_type=jnp.float32,
        )

    def norm_back(running, partial_value, source, scale, gain, width):
        scaled = partial_value * gain[None, :]
        inner = row_total(jnp.sum(scaled * source, axis=1))
        running = running + scale[:, None] * scaled - source * (scale**3 * inner / width)[:, None]
        return (running, jnp.sum(partial_value * source * scale[:, None], axis=0))

    resid = hidden_in.astype(jnp.float32)
    layer_index = 0
    scale_one = lax.rsqrt(row_total(jnp.sum(resid * resid, axis=1)) / D + epsilon)
    normed = features(
        (resid * scale_one[:, None] * norm_gains[layer_index, 0][None, :]).astype(jnp.bfloat16)
    )
    block = forward_in(normed, 0, layer_index)
    convolved, sent = conv_section(
        block, conv_weight[layer_index], conv_bias[layer_index], valid, widths
    )
    shared = lax.all_gather(sent.astype(jnp.bfloat16), "col", axis=1, tiled=True).astype(
        jnp.float32
    )
    attn, gated = mixer_core(
        block, convolved, shared, head_params[layer_index], positions, allowed, column, widths
    )
    scale_ssm = lax.rsqrt(row_total(jnp.sum(gated * gated, axis=1)) / ssm_width + epsilon)
    sout = gated * scale_ssm[:, None] * ssm_gain[layer_index][None, :]
    mixed = jnp.concatenate([attn, sout], 1).astype(jnp.bfloat16)
    after_mix = resid + feature_sum(forward_out(mixed, 0, layer_index))
    scale_two = lax.rsqrt(row_total(jnp.sum(after_mix * after_mix, axis=1)) / D + epsilon)
    normed_two = features(
        (after_mix * scale_two[:, None] * norm_gains[layer_index, 1][None, :]).astype(jnp.bfloat16)
    )
    gate_up = forward_in(normed_two, 1, layer_index)
    activated = (jax.nn.silu(gate_up[:, :ffn_cols]) * gate_up[:, ffn_cols:]).astype(jnp.bfloat16)
    next_resid = after_mix + feature_sum(forward_out(activated, 1, layer_index))
    saved = [
        (
            resid,
            scale_one,
            normed,
            block,
            convolved,
            shared,
            gated,
            scale_ssm,
            mixed,
            after_mix,
            scale_two,
            normed_two,
            gate_up,
            activated,
        )
    ]
    grad_resid = cotangent.astype(jnp.float32)
    grads_in = [None] * LAYERS
    grads_out = [None] * LAYERS
    grads_gate_up = [None] * LAYERS
    grads_down = [None] * LAYERS
    grads_gains = [None] * LAYERS
    grads_ssm_gain = [None] * LAYERS
    grads_heads = [None] * LAYERS
    grads_conv_weight = [None] * LAYERS
    grads_conv_bias = [None] * LAYERS
    for layer_index in reversed(range(LAYERS)):
        (
            source,
            scale_one,
            normed,
            block,
            convolved,
            shared,
            gated,
            scale_ssm,
            mixed,
            after_mix,
            scale_two,
            normed_two,
            gate_up,
            activated,
        ) = saved[layer_index]
        upstream = features(grad_resid.astype(jnp.bfloat16))
        grad_act = back_out(upstream, 1, layer_index)
        grads_down[layer_index] = weight_grad_cols(activated, upstream)
        gate = gate_up[:, :ffn_cols]
        upper = gate_up[:, ffn_cols:]
        sigmoid = jax.nn.sigmoid(gate)
        grad_gate = grad_act * upper * sigmoid * (1.0 + gate * (1.0 - sigmoid))
        grad_up = grad_act * gate * sigmoid
        grad_block_two = jnp.concatenate([grad_gate, grad_up], 1).astype(jnp.bfloat16)
        partial_two = feature_sum(back_in(grad_block_two, 1, layer_index))
        grads_gate_up[layer_index] = weight_grad_rows(normed_two, grad_block_two)
        grad_resid, gain_two = norm_back(
            grad_resid, partial_two, after_mix, scale_two, norm_gains[layer_index, 1], D
        )
        upstream = features(grad_resid.astype(jnp.bfloat16))
        grad_mixed = back_out(upstream, 0, layer_index)
        grads_out[layer_index] = weight_grad_cols(mixed, upstream)
        grad_attn = grad_mixed[:, :query_cols]
        grad_sout = grad_mixed[:, query_cols:]
        scaled = grad_sout * ssm_gain[layer_index][None, :]
        inner = row_total(jnp.sum(scaled * gated, axis=1))
        grad_gated = (
            scale_ssm[:, None] * scaled - gated * (scale_ssm**3 * inner / ssm_width)[:, None]
        )
        grads_ssm_gain[layer_index] = jnp.sum(grad_sout * gated * scale_ssm[:, None], axis=0)

        def core(block_in, conv_in, shared_in, params_in):
            return mixer_core(
                block_in, conv_in, shared_in, params_in, positions, allowed, column, widths
            )

        unused_core, pull_core = jax.vjp(core, block, convolved, shared, head_params[layer_index])
        grad_block_core, grad_conv, grad_shared, grad_heads = pull_core((grad_attn, grad_gated))
        grad_sent = lax.psum_scatter(
            grad_shared.astype(jnp.bfloat16), "col", scatter_dimension=1, tiled=True
        ).astype(jnp.float32)

        def section(block_in, weight_in, bias_in):
            return conv_section(block_in, weight_in, bias_in, valid, widths)

        unused_section, pull_section = jax.vjp(
            section, block, conv_weight[layer_index], conv_bias[layer_index]
        )
        grad_block_conv, grad_cweight, grad_cbias = pull_section((grad_conv, grad_sent))
        grad_block = (grad_block_core + grad_block_conv).astype(jnp.bfloat16)
        partial_one = feature_sum(back_in(grad_block, 0, layer_index))
        grads_in[layer_index] = weight_grad_rows(normed, grad_block)
        grad_resid, gain_one = norm_back(
            grad_resid, partial_one, source, scale_one, norm_gains[layer_index, 0], D
        )
        grads_gains[layer_index] = jnp.stack([gain_one, gain_two])
        grads_heads[layer_index] = grad_heads
        grads_conv_weight[layer_index] = grad_cweight
        grads_conv_bias[layer_index] = grad_cbias
    small_gains, small_ssm, small_heads, small_cweight, small_cbias = lax.psum(
        (
            jnp.stack(grads_gains),
            jnp.stack(grads_ssm_gain),
            jnp.stack(grads_heads),
            jnp.stack(grads_conv_weight),
            jnp.stack(grads_conv_bias),
        ),
        "row",
    )
    return (
        next_resid.astype(jnp.bfloat16),
        grad_resid,
        jnp.stack(grads_in),
        jnp.stack(grads_out),
        jnp.stack(grads_gate_up),
        jnp.stack(grads_down),
        small_gains,
        small_ssm,
        small_heads,
        small_cweight,
        small_cbias,
    )


def solution(mesh):
    in_specs = (
        P("row", "col"),
        P("row"),
        P("row", "col"),
        P(None, "row", "col"),
        P(None, "col", "row"),
        P(None, "row", "col"),
        P(None, "col", "row"),
        P(None, None, "col"),
        P(None, "col"),
        P(None, None, "col"),
        P(None, None, "col"),
        P(None, "col"),
    )
    out_specs = (
        P("row", "col"),
        P("row", "col"),
        P(None, "row", "col"),
        P(None, "col", "row"),
        P(None, "row", "col"),
        P(None, "col", "row"),
        P(None, None, "col"),
        P(None, "col"),
        P(None, None, "col"),
        P(None, None, "col"),
        P(None, "col"),
    )
    return jax.shard_map(
        per_device, mesh=mesh, in_specs=in_specs, out_specs=out_specs, check_vma=False
    )
```

profile of v0, /device:TPU:124, one launch (start us, length us, event | category | flops | bytes accessed | tf_op | source)
XLA Modules:
  0.0 1372.1 jit_solution(1459729698708187123)
XLA Ops:
  8.4 6.6 psum.77
  27.6 12.4 all-gather.13.cloned.1.call-done
  40.0 73.1 %all-gather.21.cloned.1.call-done = bf16[1,1024,1030]{2,1,0:T(8,128)(2,1)} async-done(((bf16[1,32,1030]{2,1,0:T(8,128)(2,1)}), bf16[1,1024,1030]{2,1,0:T(8,128)(2,1)}) %all-gather.21.cloned.1.call-update) | async-done | bytes 2109456 | tf_op jit(solution)/shard_map/all_gather | solution.py:176
  120.3 8.1 all_gather.33
  145.9 6.8 psum.78
  155.1 25.3 %all-gather.23.cloned.1.call-done = bf16[1,512,1024]{1,2,0:T(8,128)(2,1)} async-done(((bf16[1,512,32]{1,2,0:T(8,128)(2,1)}), bf16[1,512,1024]{1,2,0:T(8,128)(2,1)}) %all-gather.23.cloned.1.call-update) | async-done | bytes 1048592 | tf_op jit(solution)/shard_map/all_gather | solution.py:184
  184.4 29.0 %reduce-scatter.10.cloned.1.call-done = f32[512,256]{1,0:T(8,128)} async-done(((f32[512,1024]{1,0:T(8,128)}), f32[512,256]{1,0:T(8,128)}) %reduce-scatter.10.cloned.1.call-update) | async-done | bytes 524304 | tf_op jit(solution)/shard_map/reduce_scatter | solution.py:152
  215.3 6.9 psum.79
  226.6 58.9 %all-gather.25.cloned.1.call-done = bf16[1,1024,1024]{2,1,0:T(8,128)(2,1)} async-done(((bf16[1,32,1024]{2,1,0:T(8,128)(2,1)}), bf16[1,1024,1024]{2,1,0:T(8,128)(2,1)}) %all-gather.25.cloned.1.call-update) | async-done | bytes 2097168 | tf_op jit(solution)/shard_map/all_gather | solution.py:176
  285.5 24.7 %all-gather.15.cloned.1.call-done = bf16[512,1024]{1,0:T(8,128)(2,1)} async-done(((bf16[512,256]{1,0:T(8,128)(2,1)}), bf16[512,1024]{1,0:T(8,128)(2,1)}) %all-gather.15.cloned.1.call-update) | async-done | bytes 1048592 | tf_op jit(solution)/shard_map/all_gather | solution.py:149
  314.7 19.4 %all-gather.17.cloned.1.call-done = bf16[512,1024]{1,0:T(8,128)(2,1)} async-done(((bf16[512,256]{1,0:T(8,128)(2,1)}), bf16[512,1024]{1,0:T(8,128)(2,1)}) %all-gather.17.cloned.1.call-update) | async-done | bytes 1048592 | tf_op jit(solution)/shard_map/all_gather | solution.py:149
  334.1 67.4 %all-gather.27.cloned.1.call-done = bf16[1,512,1024]{1,2,0:T(8,128)(2,1)} async-done(((bf16[1,512,32]{1,2,0:T(8,128)(2,1)}), bf16[1,512,1024]{1,2,0:T(8,128)(2,1)}) %all-gather.27.cloned.1.call-update) | async-done | bytes 1048592 | tf_op jit(solution)/shard_map/all_gather | solution.py:184
  409.4 29.6 %reduce-scatter.14.cloned.1.call-done = f32[512,256]{1,0:T(8,128)} async-done(((f32[512,1024]{1,0:T(8,128)}), f32[512,256]{1,0:T(8,128)}) %reduce-scatter.14.cloned.1.call-update) | async-done | bytes 524304 | tf_op jit(solution)/shard_map/reduce_scatter | solution.py:152
  440.9 6.9 psum.80
  452.4 20.9 %all-gather.19.cloned.1.call-done = bf16[512,1024]{1,0:T(8,128)(2,1)} async-done(((bf16[512,256]{1,0:T(8,128)(2,1)}), bf16[512,1024]{1,0:T(8,128)(2,1)}) %all-gather.19.cloned.1.call-update) | async-done | bytes 1048592 | tf_op jit(solution)/shard_map/all_gather | solution.py:149
  476.8 7.4 psum.81
  511.8 8.8 reduce-window.29
  558.1 145.1 %reduce-scatter.26.cloned.1.call-done = bf16[512,32]{0,1:T(8,128)(2,1)} async-done(((bf16[512,1024]{0,1:T(8,128)(2,1)}), bf16[512,32]{0,1:T(8,128)(2,1)}) %reduce-scatter.26.cloned.1.call-update) | async-done | bytes 32784 | tf_op jit(solution)/shard_map/reduce_scatter | solution.py:168
  704.6 184.4 %reduce-scatter.24.cloned.1.call-done = bf16[32,1024]{1,0:T(8,128)(2,1)} async-done(((bf16[1024,1024]{1,0:T(8,128)(2,1)}), bf16[32,1024]{1,0:T(8,128)(2,1)}) %reduce-scatter.24.cloned.1.call-update) | async-done | bytes 65552 | tf_op jit(solution)/shard_map/reduce_scatter | solution.py:159
  891.4 180.7 %reduce-scatter.22.cloned.1.call-done = bf16[512,32]{0,1:T(8,128)(2,1)} async-done(((bf16[512,1024]{0,1:T(8,128)(2,1)}), bf16[512,32]{0,1:T(8,128)(2,1)}) %reduce-scatter.22.cloned.1.call-update) | async-done | bytes 32784 | tf_op jit(solution)/shard_map/reduce_scatter | solution.py:168
  1073.5 30.4 %reduce-scatter.18.cloned.1.call-done = f32[512,256]{1,0:T(8,128)} async-done(((f32[512,1024]{1,0:T(8,128)}), f32[512,256]{1,0:T(8,128)}) %reduce-scatter.18.cloned.1.call-update) | async-done | bytes 524304 | tf_op jit(solution)/shard_map/reduce_scatter | solution.py:152
  1105.2 177.3 %all-reduce.32 = (f32[1,2,256]{2,1,0:T(2,128)}, f32[1,384]{1,0:T(1,128)}, f32[1,3,6]{2,1,0:T(4,128)S(1)}, f32[1,4,448]{2,1,0:T(4,128)}, f32[1,448]{1,0:T(1,128)}) all-reduce(f32[1,2,256]{2,1,0:T(2,128)S(1)} %maximum_bitcast_fusion, f32[1,384]{1,0:T(1,128)S(1)} %stack.58, ...), channel_id=1, replica_groups=mesh['row'=32,'col'=4] {'row'}, use_global_device_ids=true, to_apply=%region_38.39 | all-reduce | flops 3154 | bytes 25232 | tf_op jit(solution)/shard_map/psum | solution.py:338
  1283.0 5.6 psum.82
  1291.1 72.5 %reduce-scatter.20.cloned.1.call-done = bf16[32,1030]{1,0:T(8,128)(2,1)} async-done(((bf16[1024,1030]{1,0:T(8,128)(2,1)}), bf16[32,1030]{1,0:T(8,128)(2,1)}) %reduce-scatter.20.cloned.1.call-update) | async-done | bytes 65936 | tf_op jit(solution)/shard_map/reduce_scatter | solution.py:159
  (444 shorter events, 147.9 us)
Async XLA Ops:
  7.2 32.8 %all-gather.13.cloned.1.call-start = ((), (), s32[]{:S(2)}) async-start(), calls=%async_computation.9 | async-start | bytes 1310720 | tf_op jit(solution)/shard_map/all_gather | solution.py:149
  18.1 95.0 %all-gather.21.cloned.1.call-start = ((), (), s32[]{:S(2)}) async-start(), calls=%async_computation.22 | async-start | bytes 2433024 | tf_op jit(solution)/shard_map/all_gather | solution.py:176
  18.8 161.6 %all-gather.23.cloned.1.call-start = ((), (), s32[]{:S(2)}) async-start(), calls=%async_computation.23 | async-start | bytes 1081344 | tf_op jit(solution)/shard_map/all_gather | solution.py:184
  19.6 193.8 %reduce-scatter.10.cloned.1.call-start = ((), (), s32[]{:S(2)}) async-start(), calls=%async_computation.10 | async-start | bytes 2621440 | tf_op jit(solution)/shard_map/reduce_scatter | solution.py:152
  183.8 101.7 %all-gather.25.cloned.1.call-start = ((), (), s32[]{:S(2)}) async-start(), calls=%async_computation.24 | async-start | bytes 2162688 | tf_op jit(solution)/shard_map/all_gather | solution.py:176
  184.4 125.8 %all-gather.15.cloned.1.call-start = ((), (), s32[]{:S(2)}) async-start(), calls=%async_computation.11 | async-start | bytes 1310720 | tf_op jit(solution)/shard_map/all_gather | solution.py:149
  224.8 109.3 %all-gather.17.cloned.1.call-start = ((), (), s32[]{:S(2)}) async-start(), calls=%async_computation.13 | async-start | bytes 1310720 | tf_op jit(solution)/shard_map/all_gather | solution.py:149
  225.6 175.9 %all-gather.27.cloned.1.call-start = ((), (), s32[]{:S(2)}) async-start(), calls=%async_computation.25 | async-start | bytes 1081344 | tf_op jit(solution)/shard_map/all_gather | solution.py:184
  226.3 212.7 %reduce-scatter.14.cloned.1.call-start = ((), (), s32[]{:S(2)}) async-start(), calls=%async_computation.14 | async-start | bytes 2621440 | tf_op jit(solution)/shard_map/reduce_scatter | solution.py:152
  409.4 64.0 %all-gather.19.cloned.1.call-start = ((), (), s32[]{:S(2)}) async-start(), calls=%async_computation.15 | async-start | bytes 1310720 | tf_op jit(solution)/shard_map/all_gather | solution.py:149
  451.1 86.2 %reduce-scatter.16.cloned.1.call-start = ((), (), s32[]{:S(2)}) async-start(), calls=%async_computation.16 | async-start | bytes 655360 | tf_op jit(solution)/shard_map/reduce_scatter | solution.py:317
  501.6 201.6 %reduce-scatter.26.cloned.1.call-start = ((), (), s32[]{:S(2)}) async-start(), calls=%async_computation.21 | async-start | bytes 1081344 | tf_op jit(solution)/shard_map/reduce_scatter | solution.py:168
  504.8 384.2 %reduce-scatter.24.cloned.1.call-start = ((), (), s32[]{:S(2)}) async-start(), calls=%async_computation.20 | async-start | bytes 2162688 | tf_op jit(solution)/shard_map/reduce_scatter | solution.py:159
  508.6 563.4 %reduce-scatter.22.cloned.1.call-start = ((), (), s32[]{:S(2)}) async-start(), calls=%async_computation.19 | async-start | bytes 1081344 | tf_op jit(solution)/shard_map/reduce_scatter | solution.py:168
  537.3 566.6 %reduce-scatter.18.cloned.1.call-start = ((), (), s32[]{:S(2)}) async-start(), calls=%async_computation.17 | async-start | bytes 2621440 | tf_op jit(solution)/shard_map/reduce_scatter | solution.py:152
  548.5 740.2 %reduce-scatter.12.cloned.1.call-start = ((), (), s32[]{:S(2)}) async-start(), calls=%async_computation.12 | async-start | bytes 2621440 | tf_op jit(solution)/shard_map/reduce_scatter | solution.py:152
  552.8 810.7 %reduce-scatter.20.cloned.1.call-start = ((), (), s32[]{:S(2)}) async-start(), calls=%async_computation.18 | async-start | bytes 2433024 | tf_op jit(solution)/shard_map/reduce_scatter | solution.py:159
  558.0 547.1 %copy-start.110 = (f32[448]{0:T(512)S(1)}, f32[448]{0:T(512)}, u32[]{:S(2)}) copy-start(f32[448]{0:T(512)} %get-tuple-element.53) | copy-start | bytes 5380
  558.0 730.6 %copy-start.96 = (f32[512]{0:T(512)S(1)}, f32[512]{0:T(512)}, u32[]{:S(2)}) copy-start(f32[512]{0:T(512)} %copy-done.95) | copy-start | bytes 6148
  558.0 730.7 %copy-start.14 = (f32[512,256]{1,0:T(8,128)S(1)}, f32[512,256]{1,0:T(8,128)}, u32[]{:S(2)}) copy-start(f32[512,256]{1,0:T(8,128)} %reduce-scatter.14.cloned.1.call-done) | copy-start | bytes 1572868
  558.1 730.7 %copy-start.35 = (bf16[512,256]{1,0:T(8,128)(2,1)S(1)}, bf16[512,256]{1,0:T(8,128)(2,1)}, u32[]{:S(2)}) copy-start(bf16[512,256]{1,0:T(8,128)(2,1)} %param.14) | copy-start | bytes 786436
  558.1 730.7 %copy-start.76 = (f32[512]{0:T(512)S(1)}, f32[512]{0:T(512)}, u32[]{:S(2)}) copy-start(f32[512]{0:T(512)} %copy-done.75) | copy-start | bytes 6148
  558.1 730.7 %copy-start.84 = (f32[1,1,256]{2,1,0:T(1,128)S(1)}, f32[1,1,256]{2,1,0:T(1,128)}, u32[]{:S(2)}) copy-start(f32[1,1,256]{2,1,0:T(1,128)} %get-tuple-element.117) | copy-start | bytes 3076
  558.1 730.7 %copy-start.86 = (f32[512]{0:T(512)S(1)}, f32[512]{0:T(512)}, u32[]{:S(2)}) copy-start(f32[512]{0:T(512)} %copy-done.85) | copy-start | bytes 6148
  (130 other events, 7049.8 us)
Sparse Core Ops, SparseCore 0:
  18.2 21.7 all-gather.12
  43.1 70.0 all-gather.20
  116.2 64.1 all-gather.22
  183.9 29.4 reduce-scatter.9
  216.9 68.5 all-gather.24
  287.7 22.4 all-gather.14
  311.9 22.1 all-gather.16
  337.6 63.8 all-gather.26
  409.5 29.4 reduce-scatter.13
  451.2 22.0 all-gather.18
  501.7 18.9 reduce-scatter.15
  522.9 180.2 reduce-scatter.25
  705.7 183.2 reduce-scatter.23
  891.2 180.8 reduce-scatter.21
  1074.5 29.3 reduce-scatter.17
  1106.1 29.7 reduce-scatter.11
  1141.4 222.1 reduce-scatter.19
where the time goes:
time: 1380 us; the launch traced here: 1370 us
  waiting for transfers between devices  977 us (71%)
  blocking collectives  226 us (16%)
  other arithmetic  69.1 us (5%)
  matrix products  61.5 us (4%)
  local copies, waits for them, and re-layouts  21.3 us (2%)
  between operations  16.2 us (1%)
    reduce_scatter x2, waiting for transfers between devices, weight_grad_cols(): lax.psum_scatter(term.astype(jnp.bfloat16), 'row', scatter_dimension=1, t...  326 us
    reduce_scatter x2, waiting for transfers between devices, weight_grad_rows(): lax.psum_scatter(term(jnp.int32(0), lax.axis_size('row') * shard_rows).as...  257 us
    psum x1, blocking collectives, per_device(): lax.psum((jnp.stack(grads_gains), jnp.stack(grads_ssm_gain), jnp.stack(gr...  177 us
    all_gather x2, waiting for transfers between devices, forward_in(): lax.all_gather(weight, 'row', axis=0, tiled=True)  132 us
    all_gather x2, waiting for transfers between devices, forward_out(): lax.all_gather(weight, 'row', axis=1, tiled=True)  92.7 us
    reduce_scatter x4, waiting for transfers between devices, feature_sum(): return lax.psum_scatter(values, 'col', scatter_dimension=1, tiled=True)  89 us
    all_gather x4, waiting for transfers between devices, features(): return lax.all_gather(values, 'col', axis=1, tiled=True)  77.4 us
    psum x6, blocking collectives, row_total(): return lax.psum(values, 'col')  40.2 us
  transfers between devices with their start and end apart: 17, of which 15 were waited for; matrix products, arithmetic and copies ran while one was open for 7% of the time, Pallas kernels for 0%

commit v1 on v0

v1 whole, which is shorter than its diff:
```python
import jax
import jax.numpy as jnp
from jax import lax
from jax.sharding import PartitionSpec as P

D = 1024
Q_HEADS = 8
KV_HEADS = 2
HEAD = 64
SSM_HEADS = 24
SSM_HEAD = 64
STATE = 128
CONV = 4
FF = 2048
LAYERS = 1


epsilon = 1e-05
rope_base = 10000.0
contract_last = (((1,), (1,)), ((), ()))
contract_first = (((0,), (0,)), ((), ()))


def lowered(value):
    rounded = lax.optimization_barrier(value.astype(jnp.bfloat16)).astype(jnp.float32)
    return value + lax.stop_gradient(rounded - value)


def sequence_masks(segments):
    length = segments.shape[0]
    index = jnp.arange(length, dtype=jnp.int32)
    previous = jnp.concatenate([segments[:1], segments[:-1]])
    starts = jnp.where(segments != previous, index, 0)
    positions = (index - lax.cummax(starts, axis=0)).astype(jnp.float32)
    allowed = (segments[:, None] == segments[None, :]) & (index[:, None] >= index[None, :])
    shifted = []
    for shift in range(CONV):
        earlier = jnp.concatenate([jnp.full((shift,), -1, jnp.int32), segments[: length - shift]])
        shifted.append((earlier == segments).astype(jnp.float32))
    return (positions, allowed, jnp.stack(shifted))


def rotate(values, positions):
    middle = values.shape[-1] // 2
    frequency = rope_base ** (-2.0 * jnp.arange(middle, dtype=jnp.float32) / values.shape[-1])
    angle = positions[:, None] * frequency[None, :]
    cosine = jnp.cos(angle)[:, None, :]
    sine = jnp.sin(angle)[:, None, :]
    first = values[..., :middle]
    second = values[..., middle:]
    return jnp.concatenate([first * cosine - second * sine, second * cosine + first * sine], -1)


def causal_conv(inner, weight, bias, valid):
    length = inner.shape[0]
    running = jnp.broadcast_to(bias[None, :], inner.shape)
    for shift in range(CONV):
        earlier = jnp.concatenate(
            [jnp.zeros((shift, inner.shape[1]), inner.dtype), inner[: length - shift]]
        )
        running = running + weight[shift][None, :] * earlier * valid[shift][:, None]
    return running


def conv_section(block, weight, bias, valid, widths):
    query_cols, ssm_cols, state_cols, head_cols = widths
    start_kv = query_cols + 2 * ssm_cols
    inner = jnp.concatenate(
        [
            block[:, query_cols + ssm_cols : start_kv],
            block[:, start_kv + HEAD : start_kv + HEAD + state_cols],
        ],
        1,
    )
    active = jax.nn.silu(causal_conv(inner, weight, bias, valid))
    sent = jnp.concatenate(
        [lowered(block[:, start_kv : start_kv + HEAD]), lowered(active[:, ssm_cols:])], 1
    )
    return (active[:, :ssm_cols], sent)


def split_shared(shared, column, widths):
    query_cols, ssm_cols, state_cols, head_cols = widths
    length = shared.shape[0]
    col_count = shared.shape[1] // (HEAD + state_cols)
    pieces = shared.reshape(length, col_count, HEAD + state_cols)
    key_index = column * KV_HEADS // col_count
    keys = lax.dynamic_index_in_dim(pieces[:, :KV_HEADS, :HEAD], key_index, 1, keepdims=False)
    values = lax.dynamic_index_in_dim(pieces[:, KV_HEADS:, :HEAD], key_index, 1, keepdims=False)
    states = pieces[:, :, HEAD:].reshape(length, col_count * state_cols)
    return (keys, values, states)


def attention_core(block, shared, positions, allowed, column, widths):
    query_cols, ssm_cols, state_cols, head_cols = widths
    length = block.shape[0]
    keys, values, states = split_shared(shared, column, widths)
    query = block[:, :query_cols].reshape(length, query_cols // HEAD, HEAD)
    qrot = lowered(rotate(query, positions))
    krot = lowered(rotate(keys[:, None, :], positions))[:, 0]
    scores = jnp.einsum("shd,td->hst", qrot, krot) * HEAD ** (-0.5)
    scores = jnp.where(allowed[None], scores, -1e30)
    top = jnp.max(scores, axis=-1, keepdims=True)
    weights = jnp.exp(scores - top)
    probs = lowered(weights / jnp.sum(weights, axis=-1, keepdims=True))
    return lowered(jnp.einsum("hst,td->shd", probs, values)).reshape(length, query_cols)


def ssm_core(block, convolved, shared, params, allowed, column, widths):
    query_cols, ssm_cols, state_cols, head_cols = widths
    length = block.shape[0]
    keys, values, states = split_shared(shared, column, widths)
    state_b = states[:, :STATE]
    state_c = states[:, STATE:]
    gate_z = block[:, query_cols : query_cols + ssm_cols]
    step_size = jax.nn.softplus(block[:, block.shape[1] - head_cols :] + params[2][None, :])
    logdecay = jnp.cumsum(step_size * (-jnp.exp(params[0]))[None, :], axis=0).T
    gram = jnp.dot(state_c, state_b.T)
    diff = logdecay[:, :, None] - logdecay[:, None, :]
    mixing = lowered(
        jnp.where(allowed[None], jnp.exp(jnp.where(allowed[None], diff, 0.0)), 0.0) * gram[None]
    )
    xin = convolved.reshape(length, head_cols, SSM_HEAD)
    inputs = lowered(step_size[:, :, None] * xin)
    ssm = jnp.einsum("hts,shp->thp", mixing, inputs) + params[1][None, :, None] * xin
    return ssm.reshape(length, ssm_cols) * jax.nn.silu(gate_z)


def swap_core(values):
    return lax.ppermute(values, "col", [(0, 1), (1, 0), (2, 3), (3, 2)])


def swap_chip(values):
    return lax.ppermute(values, "col", [(0, 2), (2, 0), (1, 3), (3, 1)])


def sum_col(values):
    values = values + swap_core(values)
    return values + swap_chip(values)


def gather_features(block, chip, core):
    other = swap_chip(block)
    pair = jnp.stack([jnp.where(chip == 0, block, other), jnp.where(chip == 0, other, block)])
    opair = swap_core(pair)
    even = jnp.where(core == 0, pair, opair)
    odd = jnp.where(core == 0, opair, pair)
    return jnp.concatenate([even[0], odd[0], even[1], odd[1]], 1)


def feature_sum(partial, chip, core):
    width = partial.shape[1] // 4
    blocks = [partial[:, i * width : (i + 1) * width] for i in range(4)]
    even = jnp.stack([blocks[0], blocks[2]])
    odd = jnp.stack([blocks[1], blocks[3]])
    sent = jnp.where(core == 0, odd, even).astype(jnp.bfloat16)
    pair = jnp.where(core == 0, even, odd) + swap_core(sent).astype(jnp.float32)
    sent = jnp.where(chip == 0, pair[1], pair[0]).astype(jnp.bfloat16)
    return jnp.where(chip == 0, pair[0], pair[1]) + swap_chip(sent).astype(jnp.float32)


def token_half(values, core):
    half = values.shape[0] // 2
    return jnp.where(core == 0, values[:half], values[half:])


def token_sum(partial, core):
    sent = token_half(partial, 1 - core).astype(jnp.bfloat16)
    pair = token_half(partial, core) + swap_core(sent).astype(jnp.float32)
    return pair + swap_chip(pair.astype(jnp.bfloat16)).astype(jnp.float32)


def token_spread(half, core):
    other = swap_core(half)
    return jnp.concatenate([jnp.where(core == 0, half, other), jnp.where(core == 0, other, half)], 0)


def per_device(
    hidden_in,
    segment_ids,
    cotangent,
    w_in,
    w_out,
    w_gate_up,
    w_down,
    norm_gains,
    ssm_gain,
    head_params,
    conv_weight,
    conv_bias,
):
    rows = lax.axis_size("row")
    col_count = lax.axis_size("col")
    column = lax.axis_index("col")
    chip = column // 2
    core = column % 2
    widths = (
        Q_HEADS * HEAD // col_count,
        SSM_HEADS * SSM_HEAD // col_count,
        2 * STATE // col_count,
        SSM_HEADS // col_count,
    )
    query_cols, ssm_cols, state_cols, head_cols = widths
    ffn_cols = FF // col_count
    ssm_width = SSM_HEADS * SSM_HEAD
    shard = w_in.shape[1]
    in_cols = w_in.shape[2]
    mix_cols = w_out.shape[1]
    bf16 = jnp.bfloat16
    f32 = jnp.float32

    def mm(left, right, dims):
        return lax.dot_general(left, right, dims, preferred_element_type=f32)

    plain = (((1,), (0,)), ((), ()))

    spread = jnp.broadcast_to(w_in[0][None], (rows, shard, in_cols))
    w_in_full = lax.all_to_all(spread, "row", 0, 0, tiled=True).reshape(rows * shard, in_cols)
    rest = jnp.concatenate([w_out[0].T, w_gate_up[0], w_down[0].T], 1)
    rest = lax.all_gather(rest, "row", axis=0, tiled=True)
    w_out_t = rest[:, :mix_cols]
    w_gu = rest[:, mix_cols : mix_cols + 2 * ffn_cols]
    w_down_t = rest[:, mix_cols + 2 * ffn_cols :]

    positions, allowed, valid = sequence_masks(segment_ids)
    gains = gather_features(norm_gains[0], chip, core)
    source = gather_features(hidden_in, chip, core).astype(f32)
    scale_one = lax.rsqrt(jnp.mean(source * source, axis=1, keepdims=True) + epsilon)
    normed = (source * scale_one * gains[0][None, :]).astype(bf16)
    upstream = gather_features(cotangent, chip, core)

    block = mm(normed, w_in_full, plain)

    def section(block_in, weight_in, bias_in):
        return conv_section(block_in, weight_in, bias_in, valid, widths)

    (convolved, sent), pull_section = jax.vjp(section, block, conv_weight[0], conv_bias[0])
    shared = gather_features(sent.astype(bf16), chip, core).astype(f32)

    def ssm(block_in, conv_in, shared_in, params_in):
        return ssm_core(block_in, conv_in, shared_in, params_in, allowed, column, widths)

    gated, pull_ssm = jax.vjp(ssm, block, convolved, shared, head_params[0])
    ssq = sum_col(jnp.sum(gated * gated, axis=1))

    def attention(block_in, shared_in):
        return attention_core(block_in, shared_in, positions, allowed, column, widths)

    attn, pull_attn = jax.vjp(attention, block, shared)
    scale_ssm = lax.rsqrt(ssq / ssm_width + epsilon)
    sout = gated * scale_ssm[:, None] * ssm_gain[0][None, :]
    mixed = jnp.concatenate([attn, sout], 1).astype(bf16)

    after_mix = token_half(source, core) + token_sum(mm(mixed, w_out_t, contract_last), core)
    scale_two = lax.rsqrt(jnp.mean(after_mix * after_mix, axis=1, keepdims=True) + epsilon)
    normed_two = token_spread((after_mix * scale_two * gains[1][None, :]).astype(bf16), core)
    gate_up = mm(normed_two, w_gu, plain)
    gate = gate_up[:, :ffn_cols]
    upper = gate_up[:, ffn_cols:]
    sigmoid = jax.nn.sigmoid(gate)
    activated = (gate * sigmoid * upper).astype(bf16)

    half_features = jnp.arange(D) // (D // 2) == chip
    kept = jnp.where(half_features[None, :], after_mix, 0.0)
    none = jnp.zeros_like(kept)
    placed = jnp.concatenate([jnp.where(core == 0, kept, none), jnp.where(core == 0, none, kept)], 0)
    hidden_out = feature_sum(mm(activated, w_down_t, contract_last) + placed, chip, core)

    grad_act = mm(upstream, w_down_t, plain)
    grad_down_t = mm(upstream, activated, contract_first)
    grad_gate = grad_act * upper * sigmoid * (1.0 + gate * (1.0 - sigmoid))
    grad_up = grad_act * gate * sigmoid
    grad_gu = jnp.concatenate([grad_gate, grad_up], 1).astype(bf16)
    partial_two = token_sum(mm(grad_gu, w_gu, contract_last), core)
    grad_w_gu = mm(normed_two, grad_gu, contract_first)
    scaled = partial_two * gains[1][None, :]
    inner = jnp.sum(scaled * after_mix, axis=1, keepdims=True)
    grad_mid = (
        token_half(upstream, core).astype(f32)
        + scale_two * scaled
        - after_mix * (scale_two**3 * inner / D)
    )
    gain_two = jnp.sum(partial_two * after_mix * scale_two, axis=0)
    gain_two = gain_two + swap_core(gain_two)
    upstream_two = token_spread(grad_mid.astype(bf16), core)

    grad_mixed = mm(upstream_two, w_out_t, plain)
    grad_out_t = mm(upstream_two, mixed, contract_first)
    grad_attn = grad_mixed[:, :query_cols]
    grad_sout = grad_mixed[:, query_cols:]
    scaled = grad_sout * ssm_gain[0][None, :]
    inner = sum_col(jnp.sum(scaled * gated, axis=1))
    grad_block_attn, grad_shared_attn = pull_attn(grad_attn)
    grad_gated = scale_ssm[:, None] * scaled - gated * (scale_ssm**3 * inner / ssm_width)[:, None]
    grad_ssm_gain = jnp.sum(grad_sout * gated * scale_ssm[:, None], axis=0)
    grad_block_ssm, grad_conv, grad_shared_ssm, grad_heads = pull_ssm(grad_gated)
    grad_sent = feature_sum(grad_shared_attn + grad_shared_ssm, chip, core)
    grad_block_conv, grad_cweight, grad_cbias = pull_section((grad_conv, grad_sent))
    grad_block = (grad_block_attn + grad_block_ssm + grad_block_conv).astype(bf16)

    partial_one = mm(grad_block, w_in_full, contract_last)
    scaled = partial_one * gains[0][None, :]
    inner = jnp.sum(scaled * source, axis=1, keepdims=True)
    kept = jnp.where(half_features[None, :], grad_mid, 0.0)
    placed = jnp.concatenate([jnp.where(core == 0, kept, none), jnp.where(core == 0, none, kept)], 0)
    grad_hidden = feature_sum(
        scale_one * scaled - source * (scale_one**3 * inner / D) + placed, chip, core
    )
    gain_one = jnp.sum(partial_one * source * scale_one, axis=0)
    gain_one = sum_col(gain_one)
    grad_w_in = mm(normed, grad_block, contract_first)

    own = lax.dynamic_slice_in_dim(jnp.stack([gain_one, gain_two]), column * (D // 4), D // 4, 1)
    pieces = (own, grad_ssm_gain, grad_heads, grad_cweight, grad_cbias)
    flat = jnp.concatenate([piece.reshape(-1) for piece in pieces])
    pad_cols = -in_cols % 128
    flat = jnp.pad(flat, (0, shard * pad_cols - flat.shape[0])).astype(bf16).reshape(shard, pad_cols)
    small = jnp.broadcast_to(flat[None], (rows, shard, pad_cols)).reshape(rows * shard, pad_cols)
    packed = jnp.concatenate(
        [
            grad_out_t.astype(bf16),
            grad_w_gu.astype(bf16),
            grad_down_t.astype(bf16),
            grad_w_in.astype(bf16),
            small,
        ],
        1,
    ).reshape(rows, shard, -1)
    packed = lax.all_to_all(packed, "row", 0, 0, tiled=True)
    total = jnp.sum(packed.astype(f32), axis=0)
    gu_end = mix_cols + 2 * ffn_cols
    down_end = gu_end + ffn_cols
    flat = total[:, down_end + in_cols :].reshape(-1)
    out_small = []
    start = 0
    for piece in pieces:
        out_small.append(flat[start : start + piece.size].reshape((1,) + piece.shape))
        start += piece.size
    return (
        hidden_out.astype(bf16),
        grad_hidden,
        total[None, :, down_end : down_end + in_cols],
        total[:, :mix_cols].T[None],
        total[None, :, mix_cols:gu_end],
        total[:, gu_end:down_end].T[None],
        *out_small,
    )


def solution(mesh):
    in_specs = (
        P("row", "col"),
        P("row"),
        P("row", "col"),
        P(None, "row", "col"),
        P(None, "col", "row"),
        P(None, "row", "col"),
        P(None, "col", "row"),
        P(None, None, "col"),
        P(None, "col"),
        P(None, None, "col"),
        P(None, None, "col"),
        P(None, "col"),
    )
    out_specs = (
        P("row", "col"),
        P("row", "col"),
        P(None, "row", "col"),
        P(None, "col", "row"),
        P(None, "row", "col"),
        P(None, "col", "row"),
        P(None, None, "col"),
        P(None, "col"),
        P(None, None, "col"),
        P(None, None, "col"),
        P(None, "col"),
    )
    return jax.shard_map(
        per_device, mesh=mesh, in_specs=in_specs, out_specs=out_specs, check_vma=False
    )
```

time: 1380 us -> 396 us (0.29)
  waiting for transfers between devices: 977 us -> 197 us
  blocking collectives: 226 us -> 0 us
  starting transfers between devices: 1.15 us -> 39.5 us
  matrix products: 61.5 us -> 43.4 us
    reduce_scatter x9 -> x0, waiting for transfers between devices: 672 us -> none  [the longest x2 326 us: weight_grad_cols(): lax.psum_scatter(term.astype(jnp.bfloat16), 'row', scatter_dimension=1, t...]
    all_gather x8 -> x1, waiting for transfers between devices: 302 us -> 31.4 us  [per_device(): rest = lax.all_gather(rest, 'row', axis=0, tiled=True)]
    psum x7 -> x0, blocking collectives: 218 us -> none  [the longest x1 177 us: per_device(): lax.psum((jnp.stack(grads_gains), jnp.stack(grads_ssm_gain), jnp.stack(gr...]
    ppermute x0 -> x27, waiting for transfers between devices: none -> 146 us  [the longest x12 141 us: swap_chip(): return lax.ppermute(values, 'col', [(0, 2), (2, 0), (1, 3), (3, 1)])]
    ppermute x0 -> x27, starting transfers between devices: none -> 20.2 us  [the longest x12 16.4 us: swap_chip(): return lax.ppermute(values, 'col', [(0, 2), (2, 0), (1, 3), (3, 1)])]
    all_to_all x0 -> x2, waiting for transfers between devices: none -> 19.4 us  [the longest x1 19.4 us: per_device(): lax.all_to_all(spread, 'row', 0, 0, tiled=True)]
    all_to_all x0 -> x2, starting transfers between devices: none -> 19.3 us  [the longest x1 9.65 us: per_device(): packed = lax.all_to_all(packed, 'row', 0, 0, tiled=True)]
    dot_general x24, matrix products: 61.5 us -> 43.4 us  [the longest x12 27.4 us: mm(): return lax.dot_general(left, right, dims, preferred_element_type=f32)]
  transfers between devices with their start and end apart: 17 -> 30, of which waited for: 15 -> 15; matrix products, arithmetic and copies ran while one was open for 7% -> 16% of each run, Pallas kernels for 0% -> 0%
where the time goes in v1:
time: 396 us; the launch traced here: 389 us
  waiting for transfers between devices  197 us (50%)
  other arithmetic  60.6 us (15%)
  matrix products  43.4 us (11%)
  starting transfers between devices  39.5 us (10%)
  local copies, waits for them, and re-layouts  31.2 us (8%)
  between operations  17.3 us (4%)
    ppermute x12, waiting for transfers between devices, swap_chip(): return lax.ppermute(values, 'col', [(0, 2), (2, 0), (1, 3), (3, 1)])  141 us
    all_gather x1, waiting for transfers between devices, per_device(): rest = lax.all_gather(rest, 'row', axis=0, tiled=True)  31.4 us
    dot_general x12, matrix products, mm(): return lax.dot_general(left, right, dims, preferred_element_type=f32)  27.4 us
    all_to_all x1, waiting for transfers between devices, per_device(): lax.all_to_all(spread, 'row', 0, 0, tiled=True)  19.4 us
    ppermute x12, starting transfers between devices, swap_chip(): return lax.ppermute(values, 'col', [(0, 2), (2, 0), (1, 3), (3, 1)])  16.4 us
    another operation x12, other arithmetic  12.1 us
    dot_general x3, matrix products, ssm_core(): jnp.einsum('hts,shp->thp', mixing, inputs) + params[1][None, :, None] * xin  11.1 us
    concatenate x1, local copies, waits for them, and re-layouts, per_device(): jnp.concatenate([grad_out_t.astype(bf16), grad_w_gu.astype(bf16), grad_do...  9.9 us
  transfers between devices with their start and end apart: 30, of which 15 were waited for; matrix products, arithmetic and copies ran while one was open for 16% of the time, Pallas kernels for 0%

profile of v1, /device:TPU:124, one launch (start us, length us, event | category | flops | bytes accessed | tf_op | source)
XLA Modules:
  0.0 388.7 jit_solution(4618306109563004257)
XLA Ops:
  9.3 2.5 broadcast_in_dim.162
  11.8 9.6 %all-to-all-start = ((bf16[32,32,1030]{2,1,0:T(8,128)(2,1)}), bf16[32,32,1030]{2,1,0:T(8,128)(2,1)}, u32[]{:S(2)}, u32[]{:S(2)}) async-start(bf16[32,32,1030]{2,1,0:T(8,128)(2,1)} %broadcast_in_dim.162), calls=%async_computation | async-start | bytes 4718592 | tf_op jit(solution)/shard_map/all_to_all | solution.py:218
  30.2 19.4 %all-to-all-done = bf16[32,32,1030]{2,1,0:T(8,128)(2,1)} async-done(((bf16[32,32,1030]{2,1,0:T(8,128)(2,1)}), bf16[32,32,1030]{2,1,0:T(8,128)(2,1)}, u32[]{:S(2)}, u32[]{:S(2)}) %all-to-all-start) | async-done | bytes 2109472 | tf_op jit(solution)/shard_map/all_to_all | solution.py:218
  49.6 3.1 fusion.68
  57.7 3.3 collective-permute-done.4
  69.7 2.8 fusion.39
  81.0 31.4 %all-gather.2.cloned.1.call-done = bf16[1024,2048]{1,0:T(8,128)(2,1)} async-done(((bf16[32,2048]{1,0:T(8,128)(2,1)}), bf16[1024,2048]{1,0:T(8,128)(2,1)}) %all-gather.2.cloned.1.call-update) | async-done | bytes 4194320 | tf_op jit(solution)/shard_map/all_gather | solution.py:220
  119.2 5.0 %collective-permute-done.13 = bf16[512,256]{1,0:T(8,128)(2,1)S(1)} collective-permute-done((bf16[512,256]{1,0:T(8,128)(2,1)S(1)}, bf16[512,256]{1,0:T(8,128)(2,1)S(1)}, u32[]{:S(2)}, u32[]{:S(2)}) %collective-permute-start.13) | collective-permute-done | bytes 262176 | tf_op jit(solution)/shard_map/ppermute | solution.py:134
  124.7 10.5 %collective-permute-done.9 = bf16[256,1024]{1,0:T(8,128)(2,1)S(1)} collective-permute-done((bf16[256,1024]{1,0:T(8,128)(2,1)S(1)}, bf16[256,1024]{1,0:T(8,128)(2,1)S(1)}, u32[]{:S(2)}, u32[]{:S(2)}) %collective-permute-start.9) | collective-permute-done | bytes 524320 | tf_op jit(solution)/shard_map/ppermute | solution.py:134
  150.3 11.2 %collective-permute-done.16 = bf16[256,1024]{1,0:T(8,128)(2,1)} collective-permute-done((bf16[256,1024]{1,0:T(8,128)(2,1)}, bf16[256,1024]{1,0:T(8,128)(2,1)}, u32[]{:S(2)}, u32[]{:S(2)}) %collective-permute-start.16) | collective-permute-done | bytes 524320 | tf_op jit(solution)/shard_map/ppermute | solution.py:134
  163.0 3.3 fusion.155
  168.9 2.6 convolution_convert_fusion.1
  187.1 3.4 multiply_reduce_fusion.10
  190.5 4.4 %fusion.6 = (f32[6,512]{1,0:T(8,128)S(1)}, f32[6,512]{1,0:T(8,128)S(1)}, bf16[512,512]{1,0:T(8,128)(2,1)S(1)}) fusion(f32[512,512]{1,0:T(8,128)S(1)} %copy-done.15, f32[6,512]{1,0:T(8,128)S(1)} %bitcast.324, pred[512,512]{1,0:T(8,128)(4,1)S(1)} %copy-done.43, f32[6,64,512]{2,1,0:T(8,128)S(1)} %bitcast.313, bf16[512,6,64]{0,2,1:T(8,128)(2,1)S(1)} %copy-done.91, ...), kind=kOutput, calls=%fused_computation.12 | convolution fusion | flops 219146240 | bytes 3850240 | tf_op jit(solution)/shard_map/transpose(jvp(hts,shp->thp))/dot_general | solution.py:125
  195.5 3.9 multiply_reduce_fusion.12
  200.6 7.6 %reduce-window.29 = f32[6,4,128]{2,1,0:T(4,128)S(1)} reduce-window(f32[6,4,128]{2,1,0:T(4,128)S(1)} %add_any.98, f32[]{:T(128)} %constant.120.clone.1), window={size=1x1x128 pad=0_0x0_0x0_127}, to_apply=%region_17.18 | reduce-window | flops 390144 | bytes 24580 | tf_op jit(solution)/shard_map/reduce-window.4
  225.0 4.8 %fusion.24 = (f32[1024]{0:T(1024)S(1)}, f32[512]{0:T(512)S(1)}, f32[512,1024]{1,0:T(8,128)}) fusion(f32[512]{0:T(512)S(1)} %copy-done.142, bf16[512,256]{1,0:T(8,128)(2,1)S(1)} %copy-done.19, bf16[512,256]{1,0:T(8,128)(2,1)S(1)} %copy-done.23, bf16[512,256]{1,0:T(8,128)(2,1)S(1)} %get-tuple-element.127, bf16[512,256]{1,0:T(8,128)(2,1)S(1)} %copy-done.27, ...), kind=kOutput, calls=%fused_computation.37 | convolution fusion | flops 1090535936 | bytes 7376896 | tf_op jit(solution)/shard_map/dot_general | solution.py:213
  229.8 2.7 convolution_convert_fusion
  234.4 3.0 copy.56
  237.8 9.9 %concatenate.142 = bf16[32,32,3200]{2,1,0:T(8,128)(2,1)} concatenate(bf16[32,32,512]{2,1,0:T(8,128)(2,1)} %bitcast.310, bf16[32,32,1024]{2,1,0:T(8,128)(2,1)} %bitcast.307, bf16[32,32,512]{2,1,0:T(8,128)(2,1)} %bitcast.309, bf16[32,32,1030]{2,1,0:T(8,128)(2,1)S(1)} %bitcast.298, bf16[32,32,122]{2,1,0:T(8,128)(2,1)S(1)} %broadcast_in_dim.183), dimensions={2} | concatenate | bytes 13107200 | tf_op jit(solution)/shard_map/concatenate | solution.py:319
  247.7 9.6 %all-to-all-start.1 = ((bf16[32,32,3200]{2,1,0:T(8,128)(2,1)}), bf16[32,32,3200]{2,1,0:T(8,128)(2,1)}, u32[]{:S(2)}, u32[]{:S(2)}) async-start(bf16[32,32,3200]{2,1,0:T(8,128)(2,1)} %concatenate.142), calls=%async_computation.1 | async-start | bytes 13107200 | tf_op jit(solution)/shard_map/all_to_all | solution.py:329
  265.4 101.1 %collective-permute-done.12 = bf16[512,256]{1,0:T(8,128)(2,1)S(1)} collective-permute-done((bf16[512,256]{1,0:T(8,128)(2,1)S(1)}, bf16[512,256]{1,0:T(8,128)(2,1)S(1)}, u32[]{:S(2)}, u32[]{:S(2)}) %collective-permute-start.12) | collective-permute-done | bytes 262176 | tf_op jit(solution)/shard_map/ppermute | solution.py:134
  367.3 3.8 collective-permute-done.23
  372.0 4.0 %convert_reduce_fusion = f32[32,3200]{1,0:T(8,128)S(1)} fusion(bf16[32,32,3200]{2,1,0:T(8,128)(2,1)} %all-to-all-done.1), kind=kLoop, calls=%fused_computation | loop fusion | flops 6451200 | bytes 6963200 | tf_op jit(solution)/shard_map/reduce_sum | solution.py:330
  (566 shorter events, 108.6 us)
Async XLA Ops:
  7.2 20.3 %collective-permute-start = (bf16[512,256]{1,0:T(8,128)(2,1)}, bf16[512,256]{1,0:T(8,128)(2,1)S(1)}, u32[]{:S(2)}, u32[]{:S(2)}) collective-permute-start(bf16[512,256]{1,0:T(8,128)(2,1)} %param.12), channel_id=1, source_target_pairs={{0,2},{2,0},{1,3},{3,1},{4,6},{6,4},{5,7},{7,5},{8,10},{10,8},{9,1... | collective-permute-start | bytes 786440 | tf_op jit(solution)/shard_map/ppermute | solution.py:134
  8.5 17.2 %collective-permute-start.2 = (f32[2,256]{1,0:T(2,128)}, f32[2,256]{1,0:T(2,128)S(1)}, u32[]{:S(2)}, u32[]{:S(2)}) collective-permute-start(f32[2,256]{1,0:T(2,128)} %bitcast.364), channel_id=1, source_target_pairs={{0,2},{2,0},{1,3},{3,1},{4,6},{6,4},{5,7},{7,5},{8,10},{10,8},{9,1... | collective-permute-start | bytes 6152 | tf_op jit(solution)/shard_map/ppermute | solution.py:134
  11.8 37.8 %all-to-all-start = ((bf16[32,32,1030]{2,1,0:T(8,128)(2,1)}), bf16[32,32,1030]{2,1,0:T(8,128)(2,1)}, u32[]{:S(2)}, u32[]{:S(2)}) async-start(bf16[32,32,1030]{2,1,0:T(8,128)(2,1)} %broadcast_in_dim.162), calls=%async_computation | async-start | bytes 4718592 | tf_op jit(solution)/shard_map/all_to_all | solution.py:218
  21.5 90.9 %all-gather.2.cloned.1.call-start = ((), (), s32[]{:S(2)}) async-start(), calls=%async_computation.2 | async-start | bytes 4325376 | tf_op jit(solution)/shard_map/all_gather | solution.py:220
  55.9 5.0 %collective-permute-start.4 = (bf16[512,128]{0,1:T(8,128)(2,1)S(1)}, bf16[512,128]{0,1:T(8,128)(2,1)S(1)}, u32[]{:S(2)}, u32[]{:S(2)}) collective-permute-start(bf16[512,128]{0,1:T(8,128)(2,1)S(1)} %pad_maximum_fusion.28), channel_id=1, source_target_pairs={{0,2},{2,0},{1,3},{3,1},{4,6},{6,4},{5,7},{7,5},{8,10},{10,8},{9,1... | collective-permute-start | bytes 393224 | tf_op jit(solution)/shard_map/ppermute | solution.py:134
  61.1 3.5 collective-permute-start.5
  75.8 3.7 collective-permute-start.7
  114.7 2.3 collective-permute-start.8
  114.8 9.3 %collective-permute-start.13 = (bf16[512,256]{1,0:T(8,128)(2,1)S(1)}, bf16[512,256]{1,0:T(8,128)(2,1)S(1)}, u32[]{:S(2)}, u32[]{:S(2)}) collective-permute-start(bf16[512,256]{1,0:T(8,128)(2,1)S(1)} %copy-done.96), channel_id=1, source_target_pairs={{0,2},{2,0},{1,3},{3,1},{4,6},{6,4},{5,7},{7,5},{8,10},{10,8},{9,1... | collective-permute-start | bytes 786440 | tf_op jit(solution)/shard_map/ppermute | solution.py:134
  117.3 17.8 %collective-permute-start.9 = (bf16[256,1024]{1,0:T(8,128)(2,1)S(1)}, bf16[256,1024]{1,0:T(8,128)(2,1)S(1)}, u32[]{:S(2)}, u32[]{:S(2)}) collective-permute-start(bf16[256,1024]{1,0:T(8,128)(2,1)S(1)} %fusion.114), channel_id=1, source_target_pairs={{0,2},{2,0},{1,3},{3,1},{4,6},{6,4},{5,7},{7,5},{8,10},{10,8},{9,1... | collective-permute-start | bytes 1572872 | tf_op jit(solution)/shard_map/ppermute | solution.py:134
  124.3 11.8 %collective-permute-start.14 = (bf16[2,512,256]{2,1,0:T(8,128)(2,1)S(1)}, bf16[2,512,256]{2,1,0:T(8,128)(2,1)S(1)}, u32[]{:S(2)}, u32[]{:S(2)}) collective-permute-start(bf16[2,512,256]{2,1,0:T(8,128)(2,1)S(1)} %pad_maximum_fusion.18), channel_id=1, source_target_pairs={{0,1},{1,0},{2,3},{3,2},{4,5},{5,4},{6,7},{7,6},{8,9},{9,8},{10,11... | collective-permute-start | bytes 1572872 | tf_op jit(solution)/shard_map/ppermute | solution.py:130
  147.0 14.5 %collective-permute-start.16 = (bf16[256,1024]{1,0:T(8,128)(2,1)}, bf16[256,1024]{1,0:T(8,128)(2,1)}, u32[]{:S(2)}, u32[]{:S(2)}) collective-permute-start(bf16[256,1024]{1,0:T(8,128)(2,1)} %get-tuple-element.70), channel_id=1, source_target_pairs={{0,2},{2,0},{1,3},{3,1},{4,6},{6,4},{5,7},{7,5},{8,10},{10,8},{9,1... | collective-permute-start | bytes 1572872 | tf_op jit(solution)/shard_map/ppermute | solution.py:134
  166.3 5.8 %collective-permute-start.17 = (bf16[256,1024]{1,0:T(8,128)(2,1)S(1)}, bf16[256,1024]{1,0:T(8,128)(2,1)S(1)}, u32[]{:S(2)}, u32[]{:S(2)}) collective-permute-start(bf16[256,1024]{1,0:T(8,128)(2,1)S(1)} %get-tuple-element.68), channel_id=1, source_target_pairs={{0,1},{1,0},{2,3},{3,2},{4,5},{5,4},{6,7},{7,6},{8,9},{9,8},{10,11... | collective-permute-start | bytes 1572872 | tf_op jit(solution)/shard_map/ppermute | solution.py:130
  168.2 3.3 collective-permute-start.26
  181.0 2.2 collective-permute-start.18
  183.2 3.8 collective-permute-start.19
  200.4 9.6 %collective-permute-start.20 = (bf16[2,512,128]{1,2,0:T(8,128)(2,1)S(1)}, bf16[2,512,128]{1,2,0:T(8,128)(2,1)}, u32[]{:S(2)}, u32[]{:S(2)}) collective-permute-start(bf16[2,512,128]{1,2,0:T(8,128)(2,1)S(1)} %select_convert_fusion.5), channel_id=1, source_target_pairs={{0,1},{1,0},{2,3},{3,2},{4,5},{5,4},{6,7},{7,6},{8,9},{9,8},{10,11... | collective-permute-start | bytes 786440 | tf_op jit(solution)/shard_map/ppermute | solution.py:130
  212.1 6.4 %collective-permute-start.21 = (bf16[512,128]{0,1:T(8,128)(2,1)}, bf16[512,128]{0,1:T(8,128)(2,1)}, u32[]{:S(2)}, u32[]{:S(2)}) collective-permute-start(bf16[512,128]{0,1:T(8,128)(2,1)} %fusion.78), channel_id=1, source_target_pairs={{0,2},{2,0},{1,3},{3,1},{4,6},{6,4},{5,7},{7,5},{8,10},{10,8},{9,1... | collective-permute-start | bytes 393224 | tf_op jit(solution)/shard_map/ppermute | solution.py:134
  229.8 2.7 collective-permute-start.24
  232.6 4.8 %collective-permute-start.25 = (f32[1024]{0:T(1024)S(1)}, f32[1024]{0:T(1024)S(1)}, u32[]{:S(2)}, u32[]{:S(2)}) collective-permute-start(f32[1024]{0:T(1024)S(1)} %add.317), channel_id=1, source_target_pairs={{0,2},{2,0},{1,3},{3,1},{4,6},{6,4},{5,7},{7,5},{8,10},{10,8},{9,1... | collective-permute-start | bytes 12296 | tf_op jit(solution)/shard_map/ppermute | solution.py:134
  247.7 124.3 %all-to-all-start.1 = ((bf16[32,32,3200]{2,1,0:T(8,128)(2,1)}), bf16[32,32,3200]{2,1,0:T(8,128)(2,1)}, u32[]{:S(2)}, u32[]{:S(2)}) async-start(bf16[32,32,3200]{2,1,0:T(8,128)(2,1)} %concatenate.142), calls=%async_computation.1 | async-start | bytes 13107200 | tf_op jit(solution)/shard_map/all_to_all | solution.py:329
  259.7 2.9 collective-permute-start.11
  262.9 103.6 %collective-permute-start.12 = (bf16[512,256]{1,0:T(8,128)(2,1)S(1)}, bf16[512,256]{1,0:T(8,128)(2,1)S(1)}, u32[]{:S(2)}, u32[]{:S(2)}) collective-permute-start(bf16[512,256]{1,0:T(8,128)(2,1)S(1)} %fusion.71), channel_id=1, source_target_pairs={{0,2},{2,0},{1,3},{3,1},{4,6},{6,4},{5,7},{7,5},{8,10},{10,8},{9,1... | collective-permute-start | bytes 786440 | tf_op jit(solution)/shard_map/ppermute | solution.py:134
  264.8 106.4 %collective-permute-start.23 = (bf16[512,256]{1,0:T(8,128)(2,1)S(1)}, bf16[512,256]{1,0:T(8,128)(2,1)S(1)}, u32[]{:S(2)}, u32[]{:S(2)}) collective-permute-start(bf16[512,256]{1,0:T(8,128)(2,1)S(1)} %fusion.72), channel_id=1, source_target_pairs={{0,2},{2,0},{1,3},{3,1},{4,6},{6,4},{5,7},{7,5},{8,10},{10,8},{9,1... | collective-permute-start | bytes 786440 | tf_op jit(solution)/shard_map/ppermute | solution.py:134
  (170 other events, 1206.5 us)
Sparse Core Ops, SparseCore 0:
  25.9 86.3 all-gather.1
